TPU v7x, 32 devices: a whole 2x2x4 slice. The times are simulated.
32 devices in a mesh: groups: 2 (over x), owner: 16 (over z, y, core), tensor: 1.
Axes of the slice: x: 2, y: 2, z: 4, core: 2. Of those that a mesh axis runs over, the one named last changes fastest.
Arguments:
- tokens: bfloat16 [6144, 4096], P(('groups', 'owner'), 'tensor'), parts along dimension 0, may hold values from -3 to 3
- cotangent: bfloat16 [6144, 1024], P(('groups', 'owner')), parts along dimension 0, may hold values from -6 to 6
- frozen_value_weight: bfloat16 [4096, 1024], P('tensor'), may hold values from -0.09375 to 0.09375
- adapter_down_weight: bfloat16 [16, 64, 4096], P('owner', None, 'tensor'), may hold values from -0.09375 to 0.09375
- adapter_up_weight: bfloat16 [16, 64, 1024], P('owner', None, 'tensor'), may hold values from -0.1875 to 0.1875
- speaker_of_clip: int32 [512], P('groups'), parts along dimension 0, may hold values from 0 to 15, as said below
Outputs:
- input_row_gradient: bfloat16 [6144, 4096], P(('groups', 'owner'), 'tensor'), parts along dimension 0
- down_grad: float32 [32, 64, 4096], P(('groups', 'owner'), None, 'tensor'), parts along dimension 0
- up_grad: float32 [32, 64, 1024], P(('groups', 'owner'), None, 'tensor'), parts along dimension 0
There are 2 independent parts, one for each index of `groups`. A program takes and returns all parts, laid end to end along the dimension named above; an argument that names none is the same for every part. Nothing has to cross between parts.
Inputs may be any that keep to these rules, and one draw needn't show every extreme that they name: `speaker_of_clip`: the clips of one device (aligned blocks of 16 entries) name no speaker more than 2 times, and one and the same speaker is named exactly 2 times in every block of a part.
All inputs are finite; a program needn't handle non-finite values.
Results may differ from a plain program's by a relative error of at most 0.0034.
Values may be sent and summed in bfloat16 or wider, within the bound.
A program may use at most 128 MiB of HBM per device.

v0:
```python
import jax
import jax.numpy as jnp
from jax import lax
from jax.sharding import PartitionSpec as P

CAP = 2


def shards(
    tokens, cotangent, frozen_value_weight, adapter_down_weight, adapter_up_weight, speaker_of_clip
):
    owners = lax.axis_size("owner")
    my_index = lax.axis_index("owner")
    core_index = lax.axis_index("tensor")
    clip_count = speaker_of_clip.shape[0] // owners
    clip_rows = tokens.shape[0] // clip_count
    model_width_half = tokens.shape[1]
    value_width_half = adapter_up_weight.shape[2]
    slot_count = owners * CAP
    contract_last = (((1,), (1,)), ((), ()))
    contract_leading = (((0,), (0,)), ((), ()))
    my_clips = lax.dynamic_slice_in_dim(speaker_of_clip, my_index * clip_count, clip_count)
    clip_order = jnp.arange(clip_count)
    earlier = (my_clips[:, None] == my_clips[None, :]) & (clip_order[None, :] < clip_order[:, None])
    position = jnp.sum(earlier.astype(jnp.int32), axis=1)
    target = my_clips * CAP + position
    placing = (jnp.arange(slot_count)[:, None] == target[None, :]).astype(jnp.bfloat16)
    value_rows = lax.dynamic_slice_in_dim(
        cotangent, core_index * value_width_half, value_width_half, 1
    )
    send_tokens = jnp.dot(
        placing, tokens.reshape(clip_count, -1), preferred_element_type=jnp.float32
    )
    send_tokens = send_tokens.astype(jnp.bfloat16).reshape(
        owners, CAP * clip_rows, model_width_half
    )
    send_values = jnp.dot(
        placing, value_rows.reshape(clip_count, -1), preferred_element_type=jnp.float32
    )
    send_values = send_values.astype(jnp.bfloat16).reshape(
        owners, CAP * clip_rows, value_width_half
    )
    got_tokens, got_values = (
        lax.all_to_all(send_tokens, "owner", split_axis=0, concat_axis=0, tiled=True),
        lax.all_to_all(send_values, "owner", split_axis=0, concat_axis=0, tiled=True),
    )
    in_rows = got_tokens.reshape(-1, model_width_half)
    in_values = got_values.reshape(-1, value_width_half)
    down_gradient_local = adapter_down_weight[0]
    up_gradient_local = adapter_up_weight[0]
    acts_part = lax.dot_general(
        down_gradient_local, in_rows, contract_last, preferred_element_type=jnp.float32
    )
    back_part = lax.dot_general(
        up_gradient_local, in_values, contract_last, preferred_element_type=jnp.float32
    )
    acts_sum, back_sum = lax.psum((acts_part, back_part), "tensor")
    acts_low = acts_sum.astype(jnp.bfloat16)
    low_rank_gradient = back_sum.astype(jnp.bfloat16)
    down_grad = jnp.dot(low_rank_gradient, in_rows, preferred_element_type=jnp.float32)[None]
    up_grad = jnp.dot(acts_low, in_values, preferred_element_type=jnp.float32)[None]
    frozen_gradient = lax.dot_general(
        cotangent, frozen_value_weight, contract_last, preferred_element_type=jnp.float32
    )
    slot_terms = lax.dot_general(
        low_rank_gradient, down_gradient_local, contract_leading, preferred_element_type=jnp.float32
    )
    slot_terms = slot_terms.astype(jnp.bfloat16).reshape(owners, CAP * clip_rows, model_width_half)
    returned = lax.all_to_all(slot_terms, "owner", split_axis=0, concat_axis=0, tiled=True)
    adapter_gradient = lax.dot_general(
        placing,
        returned.reshape(slot_count, -1),
        contract_leading,
        preferred_element_type=jnp.float32,
    )
    adapter_gradient = adapter_gradient.reshape(-1, model_width_half)
    input_row_gradient = (frozen_gradient + adapter_gradient).astype(jnp.bfloat16)
    return (input_row_gradient, down_grad, up_grad)


def solution(mesh):
    return jax.shard_map(
        shards,
        mesh=mesh,
        in_specs=(
            P(("groups", "owner"), "tensor"),
            P(("groups", "owner"), None),
            P("tensor", None),
            P("owner", None, "tensor"),
            P("owner", None, "tensor"),
            P("groups"),
        ),
        out_specs=(
            P(("groups", "owner"), "tensor"),
            P(("groups", "owner"), None, "tensor"),
            P(("groups", "owner"), None, "tensor"),
        ),
        check_vma=False,
    )
```

profile of v0, /device:TPU:13, one launch (start us, length us, event | category | flops | bytes accessed | tf_op | source)
XLA Modules:
  0.0 205.2 jit_solution(12775711121403729499)
XLA Ops:
  0.6 0.0 copy-start
  0.6 0.8 dynamic_slice.4
  1.5 0.2 convert_reduce_fusion
  1.6 0.8 multiply_add_fusion
  2.4 1.6 reshape.36
  4.0 0.3 convolution_convert_fusion.1
  4.3 2.1 %reshape.37 = bf16[16,24,1024]{2,1,0:T(8,128)(2,1)} reshape(bf16[32,12288]{1,0:T(8,128)(2,1)S(1)} %convolution_convert_fusion.1) | data formatting | bytes 1572864 | tf_op jit(solution)/shard_map/reshape | solution.py:40
  6.4 6.6 %all-to-all-start = ((bf16[16,24,1024]{2,1,0:T(8,128)(2,1)}), bf16[16,24,1024]{2,1,0:T(8,128)(2,1)S(1)}, u32[]{:S(2)}, u32[]{:S(2)}) async-start(bf16[16,24,1024]{2,1,0:T(8,128)(2,1)} %reshape.37), calls=%async_computation | async-start | bytes 1572864 | tf_op jit(solution)/shard_map/all_to_all | solution.py:45
  13.0 3.5 %reshape.42 = bf16[16,49152]{1,0:T(8,128)(2,1)S(1)} reshape(bf16[192,4096]{1,0:T(8,128)(2,1)} %param.6) | data formatting | bytes 3145728 | tf_op jit(solution)/shard_map/reshape | solution.py:32
  16.5 2.6 %convolution_convert_fusion = bf16[32,49152]{1,0:T(8,128)(2,1)} fusion(bf16[16,49152]{1,0:T(8,128)(2,1)S(1)} %reshape.42, s32[16]{0:T(128)S(1)} %multiply_add_fusion), kind=kOutput, calls=%fused_computation | convolution fusion | flops 51905024 | bytes 4718656 | tf_op jit(solution)/shard_map/dot_general | solution.py:31
  19.2 7.1 %reshape.43 = bf16[16,24,4096]{2,1,0:T(8,128)(2,1)} reshape(bf16[32,49152]{1,0:T(8,128)(2,1)} %convolution_convert_fusion) | data formatting | bytes 6291456 | tf_op jit(solution)/shard_map/reshape | solution.py:34
  26.2 5.9 %all-to-all-done = bf16[16,24,1024]{2,1,0:T(8,128)(2,1)S(1)} async-done(((bf16[16,24,1024]{2,1,0:T(8,128)(2,1)}), bf16[16,24,1024]{2,1,0:T(8,128)(2,1)S(1)}, u32[]{:S(2)}, u32[]{:S(2)}) %all-to-all-start) | async-done | bytes 786464 | tf_op jit(solution)/shard_map/all_to_all | solution.py:45
  32.2 5.0 %all-to-all-start.2 = ((bf16[16,24,4096]{2,1,0:T(8,128)(2,1)}), bf16[16,24,4096]{2,1,0:T(8,128)(2,1)}, u32[]{:S(2)}, u32[]{:S(2)}) async-start(bf16[16,24,4096]{2,1,0:T(8,128)(2,1)} %reshape.43), calls=%async_computation.2 | async-start | bytes 6291456 | tf_op jit(solution)/shard_map/all_to_all | solution.py:44
  37.2 0.4 convolution_convert_fusion.4
  37.5 2.7 %convolution_convert_fusion.2 = bf16[384,4096]{1,0:T(8,128)(2,1)} fusion(bf16[384,64]{0,1:T(8,128)(2,1)S(1)} %convolution_convert_fusion.4, bf16[1,64,4096]{2,1,0:T(8,128)(2,1)S(1)} %copy-done), kind=kOutput, calls=%fused_computation.2 | convolution fusion | flops 202899456 | bytes 3719168 | tf_op jit(solution)/shard_map/dot_general | solution.py:65
  40.2 66.9 %all-to-all-done.2 = bf16[16,24,4096]{2,1,0:T(8,128)(2,1)} async-done(((bf16[16,24,4096]{2,1,0:T(8,128)(2,1)}), bf16[16,24,4096]{2,1,0:T(8,128)(2,1)}, u32[]{:S(2)}, u32[]{:S(2)}) %all-to-all-start.2) | async-done | bytes 3145760 | tf_op jit(solution)/shard_map/all_to_all | solution.py:44
  107.1 4.9 %all-to-all-start.1 = ((bf16[16,24,4096]{2,1,0:T(8,128)(2,1)}), bf16[16,24,4096]{2,1,0:T(8,128)(2,1)}, u32[]{:S(2)}, u32[]{:S(2)}) async-start(bf16[16,24,4096]{2,1,0:T(8,128)(2,1)} %bitcast.27), calls=%async_computation.1 | async-start | bytes 6291456 | tf_op jit(solution)/shard_map/all_to_all | solution.py:69
  112.1 3.5 %convolution_bitcast_fusion = f32[1,64,4096]{2,1,0:T(8,128)} fusion(bf16[384,64]{0,1:T(8,128)(2,1)S(1)} %convolution_convert_fusion.4, bf16[384,4096]{1,0:T(8,128)(2,1)} %bitcast.4), kind=kOutput, calls=%fused_computation.5 | convolution fusion | flops 201326592 | bytes 4243456 | tf_op jit(solution)/shard_map/dot_general | solution.py:60
  115.6 4.0 %convolution_bitcast_fusion.1 = f32[1,64,1024]{2,1,0:T(8,128)} fusion(bf16[384,1024]{1,0:T(8,128)(2,1)S(1)} %bitcast.29, bf16[384,4096]{1,0:T(8,128)(2,1)} %bitcast.4, bf16[1,64,4096]{2,1,0:T(8,128)(2,1)S(1)} %copy-done), kind=kOutput, calls=%fused_computation.6 | convolution fusion | flops 251682816 | bytes 4718592 | tf_op jit(solution)/shard_map/dot_general | solution.py:61
  119.6 62.5 %all-to-all-done.1 = bf16[16,24,4096]{2,1,0:T(8,128)(2,1)} async-done(((bf16[16,24,4096]{2,1,0:T(8,128)(2,1)}), bf16[16,24,4096]{2,1,0:T(8,128)(2,1)}, u32[]{:S(2)}, u32[]{:S(2)}) %all-to-all-start.1) | async-done | bytes 3145760 | tf_op jit(solution)/shard_map/all_to_all | solution.py:69
  182.1 7.1 %reshape.40 = bf16[32,49152]{1,0:T(8,128)(2,1)} reshape(bf16[16,24,4096]{2,1,0:T(8,128)(2,1)} %all-to-all-done.1) | data formatting | bytes 6291456 | tf_op jit(solution)/shard_map/reshape | solution.py:72
  189.1 4.2 %fusion.5 = f32[16,49152]{1,0:T(8,128)} fusion(bf16[32,49152]{1,0:T(8,128)(2,1)} %reshape.40, s32[16]{0:T(128)S(1)} %multiply_add_fusion), kind=kOutput, calls=%fused_computation.13 | convolution fusion | flops 50332160 | bytes 6291520 | tf_op jit(solution)/shard_map/dot_general | solution.py:70
  193.3 3.6 %reshape.41 = f32[192,4096]{1,0:T(8,128)} reshape(f32[16,49152]{1,0:T(8,128)} %fusion.5) | data formatting | bytes 6291456 | tf_op jit(solution)/shard_map/reshape | solution.py:76
  196.9 8.3 %fusion = bf16[192,4096]{1,0:T(8,128)(2,1)} fusion(f32[192,4096]{1,0:T(8,128)} %reshape.41, bf16[192,1024]{1,0:T(8,128)(2,1)S(1)} %copy-done.1, bf16[4096,1024]{1,0:T(8,128)(2,1)} %param.8), kind=kOutput, calls=%fused_computation.4 | convolution fusion | flops 1612185600 | bytes 13500416 | tf_op jit(solution)/shard_map/dot_general | solution.py:62
  (5 shorter events, 0.0 us)
Async XLA Ops:
  0.6 36.9 %copy-start = (bf16[1,64,4096]{2,1,0:T(8,128)(2,1)S(1)}, bf16[1,64,4096]{2,1,0:T(8,128)(2,1)}, u32[]{:S(2)}) copy-start(bf16[1,64,4096]{2,1,0:T(8,128)(2,1)} %param.9) | copy-start | bytes 1572868
  6.4 25.8 %all-to-all-start = ((bf16[16,24,1024]{2,1,0:T(8,128)(2,1)}), bf16[16,24,1024]{2,1,0:T(8,128)(2,1)S(1)}, u32[]{:S(2)}, u32[]{:S(2)}) async-start(bf16[16,24,1024]{2,1,0:T(8,128)(2,1)} %reshape.37), calls=%async_computation | async-start | bytes 1572864 | tf_op jit(solution)/shard_map/all_to_all | solution.py:45
  26.2 10.9 %copy-start.2 = (bf16[1,64,1024]{2,1,0:T(8,128)(2,1)S(1)}, bf16[1,64,1024]{2,1,0:T(8,128)(2,1)}, u32[]{:S(2)}) copy-start(bf16[1,64,1024]{2,1,0:T(8,128)(2,1)} %param.10) | copy-start | bytes 393220
  32.2 74.9 %all-to-all-start.2 = ((bf16[16,24,4096]{2,1,0:T(8,128)(2,1)}), bf16[16,24,4096]{2,1,0:T(8,128)(2,1)}, u32[]{:S(2)}, u32[]{:S(2)}) async-start(bf16[16,24,4096]{2,1,0:T(8,128)(2,1)} %reshape.43), calls=%async_computation.2 | async-start | bytes 6291456 | tf_op jit(solution)/shard_map/all_to_all | solution.py:44
  107.1 74.9 %all-to-all-start.1 = ((bf16[16,24,4096]{2,1,0:T(8,128)(2,1)}), bf16[16,24,4096]{2,1,0:T(8,128)(2,1)}, u32[]{:S(2)}, u32[]{:S(2)}) async-start(bf16[16,24,4096]{2,1,0:T(8,128)(2,1)} %bitcast.27), calls=%async_computation.1 | async-start | bytes 6291456 | tf_op jit(solution)/shard_map/all_to_all | solution.py:69
  193.3 3.6 %copy-start.1 = (bf16[192,1024]{1,0:T(8,128)(2,1)S(1)}, bf16[192,1024]{1,0:T(8,128)(2,1)}, u32[]{:S(2)}) copy-start(bf16[192,1024]{1,0:T(8,128)(2,1)} %param.7) | copy-start | bytes 1179652
where the time goes:
time: 206 us; the launch traced here: 205 us
  waiting for transfers between devices  135 us (66%)
  matrix products  26 us (13%)
  local copies, waits for them, and re-layouts  25.8 us (13%)
  starting transfers between devices  16.4 us (8%)
    all_to_all x1, waiting for transfers between devices, shards(): lax.all_to_all(send_tokens, 'owner', split_axis=0, concat_axis=0, tiled=T...  66.9 us
    all_to_all x1, waiting for transfers between devices, shards(): lax.all_to_all(slot_terms, 'owner', split_axis=0, concat_axis=0, tiled=True)  62.5 us
    dot_general x1, matrix products, shards(): lax.dot_general(cotangent, frozen_value_weight, contract_last, preferred_...  8.33 us
    reshape x1, local copies, waits for them, and re-layouts, shards(): send_tokens.astype(jnp.bfloat16)  7.09 us
    reshape x1, local copies, waits for them, and re-layouts, shards(): returned.reshape(slot_count, -1)  7.09 us
    all_to_all x1, starting transfers between devices, shards(): lax.all_to_all(send_values, 'owner', split_axis=0, concat_axis=0, tiled=T...  6.56 us
    all_to_all x1, waiting for transfers between devices, shards(): lax.all_to_all(send_values, 'owner', split_axis=0, concat_axis=0, tiled=T...  5.95 us
    all_to_all x1, starting transfers between devices, shards(): lax.all_to_all(send_tokens, 'owner', split_axis=0, concat_axis=0, tiled=T...  4.95 us
  transfers between devices with their start and end apart: 3, of which 3 were waited for; matrix products, arithmetic and copies ran while one was open for 12% of the time, Pallas kernels for 0%

commit v1 on v0

--- a/solution.py
+++ b/solution.py
@@ -1,6 +1,10 @@
+import functools
+
 import jax
 import jax.numpy as jnp
 from jax import lax
+from jax.experimental import pallas as pl
+from jax.experimental.pallas import tpu as pltpu
 from jax.sharding import PartitionSpec as P
 
 CAP = 2
@@ -78,9 +82,361 @@
     return (input_row_gradient, down_grad, up_grad)
 
 
+PLANE = 4
+MESH = pl.DeviceIdType.MESH
+NT = (((1,), (1,)), ((), ()))
+
+
+def dot(a, b):
+    return jnp.dot(a, b, preferred_element_type=jnp.float32)
+
+
+def slot_starts(clips_ref, first, clip_count, clip_rows, layers, block):
+    speakers = [clips_ref[first + j] for j in range(clip_count)]
+    starts = []
+    for j in range(clip_count):
+        position = jnp.int32(0)
+        for i in range(j):
+            position = position + jnp.where(speakers[i] == speakers[j], 1, 0)
+        speaker = speakers[j]
+        column = lax.rem(speaker, PLANE)
+        layer = lax.div(speaker, PLANE)
+        starts.append(column * block + layer * (CAP * clip_rows) + position * clip_rows)
+    return starts
+
+
+def placed_rows(starts, shape, dim, clip_rows):
+    token = lax.broadcasted_iota(jnp.int32, shape, dim)
+    clip = lax.div(token, clip_rows)
+    target = lax.rem(token, clip_rows)
+    for j, start in enumerate(starts):
+        target = target + jnp.where(clip == j, start, 0)
+    return target
+
+
+def kernel(
+    layers,
+    clip_count,
+    clip_rows,
+    chunks,
+    clips_ref,
+    tokens_ref,
+    cotangent_ref,
+    down_ref,
+    up_ref,
+    frozen_ref,
+    out_ref,
+    down_grad_ref,
+    up_grad_ref,
+    frozen,
+    place,
+    unplace,
+    send_t,
+    send_c,
+    got_t,
+    got_c,
+    all_down,
+    all_up,
+    low,
+    low_t,
+    acts,
+    terms,
+    back,
+    send_g,
+    got_g,
+    send_u,
+    got_u,
+    base,
+    frozen_sem,
+    t_sem,
+    c_sem,
+    d_sem,
+    u_sem,
+    r_sem,
+    g_sem,
+    v_sem,
+):
+    me = lax.axis_index("owner")
+    column = me % PLANE
+    layer = me // PLANE
+    rows = tokens_ref.shape[0]
+    width = tokens_ref.shape[1] // chunks
+    rank = down_ref.shape[0]
+    block = layers * CAP * clip_rows
+    slots = PLANE * block
+    all_rank = layers * rank
+
+    frozen_copy = pltpu.make_async_copy(frozen_ref, frozen, frozen_sem)
+    frozen_copy.start()
+
+    def in_plane(j):
+        return layer * PLANE + (column + j) % PLANE
+
+    def in_line(j):
+        return ((layer + j) % layers) * PLANE + column
+
+    barrier = pltpu.get_barrier_semaphore()
+    for j in range(1, PLANE):
+        pl.semaphore_signal(barrier, inc=1, device_id={"owner": in_plane(j)}, device_id_type=MESH)
+    for j in range(1, layers):
+        pl.semaphore_signal(barrier, inc=1, device_id={"owner": in_line(j)}, device_id_type=MESH)
+    pl.semaphore_wait(barrier, PLANE - 1 + layers - 1)
+
+    def remote(src, dst, sems, at, owner):
+        return pltpu.make_async_remote_copy(
+            src_ref=src,
+            dst_ref=dst,
+            send_sem=sems.at[(0,) + at],
+            recv_sem=sems.at[(1,) + at],
+            device_id={"owner": owner},
+            device_id_type=MESH,
+        )
+
+    def span(k):
+        return pl.ds(pl.multiple_of(k * width, width), width)
+
+    def up_copy(j):
+        return remote(up_ref, all_up.at[layer], u_sem, (j,), in_line(j))
+
+    def down_copy(k, j):
+        return remote(
+            down_ref.at[:, span(k)], all_down.at[k, layer], d_sem, (k, j), in_line(j)
+        )
+
+    def value_copy(j):
+        return remote(
+            send_c.at[(column + j) % PLANE], got_c.at[column], c_sem, (j,), in_plane(j)
+        )
+
+    def token_copy(k, j):
+        return remote(
+            send_t.at[k, (column + j) % PLANE], got_t.at[k, column], t_sem, (k, j), in_plane(j)
+        )
+
+    def term_copy(k, j):
+        return remote(
+            terms.at[k, (column + j) % PLANE], back.at[k, column], r_sem, (k, j), in_plane(j)
+        )
+
+    def grad_copy(k, j):
+        return remote(
+            send_g.at[k, (layer + j) % layers], got_g.at[k, j], g_sem, (k, j), in_line(j)
+        )
+
+    def up_grad_copy(j):
+        return remote(send_u.at[(layer + j) % layers], got_u.at[j], v_sem, (j,), in_line(j))
+
+    for j in range(1, layers):
+        up_copy(j).start()
+
+    starts = slot_starts(clips_ref, me * clip_count, clip_count, clip_rows, layers, block)
+    slot = lax.broadcasted_iota(jnp.int32, (slots, rows), 0)
+    target = placed_rows(starts, (slots, rows), 1, clip_rows)
+    place[...] = jnp.where(slot == target, 1.0, 0.0).astype(jnp.bfloat16)
+    slot = lax.broadcasted_iota(jnp.int32, (rows, slots), 1)
+    target = placed_rows(starts, (rows, slots), 0, clip_rows)
+    unplace[...] = jnp.where(slot == target, 1.0, 0.0).astype(jnp.bfloat16)
+
+    send_c[...] = (
+        dot(place[...], cotangent_ref[...]).astype(jnp.bfloat16).reshape(send_c.shape)
+    )
+    for j in range(1, PLANE):
+        value_copy(j).start()
+
+    @pl.loop(0, chunks)
+    def _(k):
+        for j in range(1, layers):
+            down_copy(k, j).start()
+        placed = dot(place[...], tokens_ref[:, span(k)]).astype(jnp.bfloat16)
+        send_t[k] = placed.reshape(PLANE, block, width)
+        for j in range(1, PLANE):
+            token_copy(k, j).start()
+        got_t[k, column] = send_t[k, column]
+        all_down[k, layer] = down_ref[:, span(k)]
+
+    got_c[column] = send_c[column]
+    all_up[layer] = up_ref[...]
+    frozen_copy.wait()
+
+    @pl.loop(0, chunks)
+    def _(k):
+        base[k] = lax.dot_general(
+            cotangent_ref[...],
+            frozen[span(k), :],
+            NT,
+            preferred_element_type=jnp.float32,
+        )
+
+    for j in range(1, layers):
+        up_copy(j).wait_recv()
+    for j in range(1, PLANE):
+        value_copy(j).wait_recv()
+
+    def own(shape, slot_dim, rank_dim):
+        slot_layer = lax.div(
+            lax.rem(lax.broadcasted_iota(jnp.int32, shape, slot_dim), block), CAP * clip_rows
+        )
+        return slot_layer == lax.div(lax.broadcasted_iota(jnp.int32, shape, rank_dim), rank)
+
+    values = got_c[...].reshape(slots, got_c.shape[2])
+    ups = all_up[...].reshape(all_rank, all_up.shape[2])
+    full = lax.dot_general(values, ups, NT, preferred_element_type=jnp.float32)
+    low[...] = jnp.where(own((slots, all_rank), 0, 1), full, 0.0).astype(jnp.bfloat16)
+    full = lax.dot_general(ups, values, NT, preferred_element_type=jnp.float32)
+    low_t[...] = jnp.where(own((all_rank, slots), 1, 0), full, 0.0).astype(jnp.bfloat16)
+    acts[...] = jnp.zeros_like(acts)
+
+    @pl.loop(0, chunks)
+    def _(k):
+        for j in range(1, layers):
+            down_copy(k, j).wait_recv()
+        downs = all_down[k].reshape(all_rank, width)
+        term = dot(low[...], downs).astype(jnp.bfloat16).reshape(PLANE, block, width)
+        terms[k] = term
+        for j in range(1, PLANE):
+            term_copy(k, j).start()
+        back[k, column] = terms[k, column]
+        for j in range(1, PLANE):
+            token_copy(k, j).wait_recv()
+        tokens = got_t[k].reshape(slots, width)
+        grad = dot(low_t[...], tokens).reshape(layers, rank, width)
+        send_g[k] = grad.astype(jnp.bfloat16)
+        for j in range(1, layers):
+            grad_copy(k, j).start()
+        down_grad_ref[:, span(k)] = lax.dot_general(
+            low_t[pl.ds(pl.multiple_of(layer * rank, rank), rank), :],
+            tokens,
+            (((1,), (0,)), ((), ())),
+            preferred_element_type=jnp.float32,
+        )
+        acts[...] += lax.dot_general(downs, tokens, NT, preferred_element_type=jnp.float32)
+
+    acts_low = jnp.where(own((all_rank, slots), 1, 0), acts[...], 0.0).astype(jnp.bfloat16)
+    grad = dot(acts_low, got_c[...].reshape(slots, got_c.shape[2]))
+    base_u = grad.reshape(layers, rank, got_c.shape[2])
+    send_u[...] = base_u.astype(jnp.bfloat16)
+    for j in range(1, layers):
+        up_grad_copy(j).start()
+    mine = jnp.zeros((rank, got_c.shape[2]), jnp.float32)
+    for i in range(layers):
+        mine = jnp.where(layer == i, base_u[i], mine)
+    up_grad_ref[...] = mine
+
+    @pl.loop(0, chunks)
+    def _(k):
+        for j in range(1, PLANE):
+            term_copy(k, j).wait_recv()
+        returned = dot(unplace[...], back[k].reshape(slots, width))
+        out_ref[:, span(k)] = (base[k] + returned).astype(jnp.bfloat16)
+
+    @pl.loop(0, chunks)
+    def _(k):
+        total = down_grad_ref[:, span(k)]
+        for j in range(1, layers):
+            grad_copy(k, j).wait_recv()
+            total = total + got_g[k, j].astype(jnp.float32)
+        down_grad_ref[:, span(k)] = total
+
+    total = up_grad_ref[...]
+    for j in range(1, layers):
+        up_grad_copy(j).wait_recv()
+        total = total + got_u[j].astype(jnp.float32)
+    up_grad_ref[...] = total
+
+    for j in range(1, layers):
+        up_copy(j).wait_send()
+        up_grad_copy(j).wait_send()
+    for j in range(1, PLANE):
+        value_copy(j).wait_send()
+
+    @pl.loop(0, chunks)
+    def _(k):
+        for j in range(1, layers):
+            down_copy(k, j).wait_send()
+            grad_copy(k, j).wait_send()
+        for j in range(1, PLANE):
+            token_copy(k, j).wait_send()
+            term_copy(k, j).wait_send()
+
+
+def fused(
+    tokens, cotangent, frozen_value_weight, adapter_down_weight, adapter_up_weight, speaker_of_clip
+):
+    owners = lax.axis_size("owner")
+    layers = owners // PLANE
+    clip_count = speaker_of_clip.shape[0] // owners
+    rows, model_width = tokens.shape
+    value_width = cotangent.shape[1]
+    clip_rows = rows // clip_count
+    rank = adapter_down_weight.shape[1]
+    chunks = 8
+    width = model_width // chunks
+    block = layers * CAP * clip_rows
+    slots = PLANE * block
+    half = jnp.bfloat16
+    vmem = pl.BlockSpec(memory_space=pltpu.VMEM)
+    dma = pltpu.SemaphoreType.DMA
+    out, down_grad, up_grad = pl.pallas_call(
+        functools.partial(kernel, layers, clip_count, clip_rows, chunks),
+        out_shape=(
+            jax.ShapeDtypeStruct((rows, model_width), half),
+            jax.ShapeDtypeStruct((rank, model_width), jnp.float32),
+            jax.ShapeDtypeStruct((rank, value_width), jnp.float32),
+        ),
+        in_specs=[pl.BlockSpec(memory_space=pltpu.SMEM)]
+        + [vmem] * 4
+        + [pl.BlockSpec(memory_space=pl.ANY)],
+        out_specs=(vmem, vmem, vmem),
+        scratch_shapes=[
+            pltpu.VMEM((model_width, value_width), half),
+            pltpu.VMEM((slots, rows), half),
+            pltpu.VMEM((rows, slots), half),
+            pltpu.VMEM((chunks, PLANE, block, width), half),
+            pltpu.VMEM((PLANE, block, value_width), half),
+            pltpu.VMEM((chunks, PLANE, block, width), half),
+            pltpu.VMEM((PLANE, block, value_width), half),
+            pltpu.VMEM((chunks, layers, rank, width), half),
+            pltpu.VMEM((layers, rank, value_width), half),
+            pltpu.VMEM((slots, layers * rank), half),
+            pltpu.VMEM((layers * rank, slots), half),
+            pltpu.VMEM((layers * rank, slots), jnp.float32),
+            pltpu.VMEM((chunks, PLANE, block, width), half),
+            pltpu.VMEM((chunks, PLANE, block, width), half),
+            pltpu.VMEM((chunks, layers, rank, width), half),
+            pltpu.VMEM((chunks, layers, rank, width), half),
+            pltpu.VMEM((layers, rank, value_width), half),
+            pltpu.VMEM((layers, rank, value_width), half),
+            pltpu.VMEM((chunks, rows, width), jnp.float32),
+            dma(()),
+            dma((2, chunks, PLANE)),
+            dma((2, PLANE)),
+            dma((2, chunks, layers)),
+            dma((2, layers)),
+            dma((2, chunks, PLANE)),
+            dma((2, chunks, layers)),
+            dma((2, layers)),
+        ],
+        compiler_params=pltpu.CompilerParams(
+            collective_id=0, has_side_effects=True, vmem_limit_bytes=56 * 2**20
+        ),
+        cost_estimate=pl.CostEstimate(
+            flops=8 * 10**9, bytes_accessed=16 * 2**20, transcendentals=0
+        ),
+    )(
+        speaker_of_clip,
+        tokens,
+        cotangent,
+        adapter_down_weight[0],
+        adapter_up_weight[0],
+        frozen_value_weight,
+    )
+    return out, down_grad[None], up_grad[None]
+
+
 def solution(mesh):
+    body = fused if mesh.shape["tensor"] == 1 and mesh.shape["owner"] == 16 else shards
     return jax.shard_map(
-        shards,
+        body,
         mesh=mesh,
         in_specs=(
             P(("groups", "owner"), "tensor"),

time: 206 us -> 128 us (0.62)
  the two profiles are of different devices: /device:TPU:13 before, /device:TPU:1 now
where the time goes in v1:
time: 128 us; the launch traced here: 127 us
  Pallas kernels  121 us (95%)
  local copies, waits for them, and re-layouts  4.59 us (4%)
    pallas_call x1, Pallas kernels, fused(): pl.pallas_call(functools.partial(kernel, layers, clip_count, clip_rows, c...  121 us
    unnamed x7, local copies, waits for them, and re-layouts  4.59 us

profile of v1, /device:TPU:1, one launch (start us, length us, event | category | flops | bytes accessed | tf_op | source)
XLA Modules:
  0.0 126.5 jit_solution(2320976532381578985)
XLA Ops:
  0.6 121.3 %shard_map.85 = (bf16[192,4096]{1,0:T(8,128)(2,1)}, f32[64,4096]{1,0:T(8,128)}, f32[64,1024]{1,0:T(8,128)}) custom-call(s32[256]{0:T(256)} %clips_ref.1, bf16[192,4096]{1,0:T(8,128)(2,1)} %tokens_ref.1, bf16[192,1024]{1,0:T(8,128)(2,1)} %cotangent_ref.1, bf16[64,4096]{1,0:T(8,128)(2,1)} %bitcast.6, bf16[64,1024]{1,0:T(8,128)(2,1)} %bitcast.7, ...), custom_call_target="tpu_custom_call" | custom-call | flops 8000000000 | bytes 16777216 | tf_op jit(solution)/shard_map/pallas_call | solution.py:379
  121.9 0.0 copy-start
  121.9 2.8 %copy.12 = bf16[192,4096]{1,0:T(8,128)(2,1)} copy(bf16[192,4096]{1,0:T(8,128)(2,1)} %get-tuple-element.12) | data formatting | bytes 3145728
  124.7 0.0 copy-done
  124.7 0.0 copy-start.1
  124.7 1.0 copy.13
  125.7 0.1 copy-done.1
  125.8 0.7 copy.14
Async XLA Ops:
  121.9 2.8 %copy-start = (f32[64,4096]{1,0:T(8,128)S(1)}, f32[64,4096]{1,0:T(8,128)}, u32[]{:S(2)}) copy-start(f32[64,4096]{1,0:T(8,128)} %get-tuple-element.7) | copy-start | bytes 3145732
  124.7 1.1 copy-start.1

commit v2 on v1

--- a/solution.py
+++ b/solution.py
@@ -83,6 +83,8 @@
 
 
 PLANE = 4
+AHEAD = 2
+LAG = 2
 MESH = pl.DeviceIdType.MESH
 NT = (((1,), (1,)), ((), ()))
 
@@ -142,10 +144,17 @@
     acts,
     terms,
     back,
+    grad,
+    keep,
     send_g,
     got_g,
+    far_g,
+    in_g,
+    keep_u,
     send_u,
     got_u,
+    far_u,
+    in_u,
     base,
     frozen_sem,
     t_sem,
@@ -154,11 +163,20 @@
     u_sem,
     r_sem,
     g_sem,
+    h_sem,
     v_sem,
+    w_sem,
+    x_sem,
+    y_sem,
 ):
     me = lax.axis_index("owner")
+    group = lax.axis_index("groups")
     column = me % PLANE
     layer = me // PLANE
+    carrier = column % 2 == group
+    pair = layer + 1 - 2 * (layer % 2)
+    far = (layer + 2) % layers
+    pair_far = (pair + 2) % layers
     rows = tokens_ref.shape[0]
     width = tokens_ref.shape[1] // chunks
     rank = down_ref.shape[0]
@@ -180,7 +198,9 @@
         pl.semaphore_signal(barrier, inc=1, device_id={"owner": in_plane(j)}, device_id_type=MESH)
     for j in range(1, layers):
         pl.semaphore_signal(barrier, inc=1, device_id={"owner": in_line(j)}, device_id_type=MESH)
-    pl.semaphore_wait(barrier, PLANE - 1 + layers - 1)
+    across = {"groups": 1 - group, "owner": me}
+    pl.semaphore_signal(barrier, inc=1, device_id=across, device_id_type=MESH)
+    pl.semaphore_wait(barrier, PLANE - 1 + layers - 1 + 1)
 
     def remote(src, dst, sems, at, owner):
         return pltpu.make_async_remote_copy(
@@ -218,16 +238,45 @@
             terms.at[k, (column + j) % PLANE], back.at[k, column], r_sem, (k, j), in_plane(j)
         )
 
-    def grad_copy(k, j):
-        return remote(
-            send_g.at[k, (layer + j) % layers], got_g.at[k, j], g_sem, (k, j), in_line(j)
-        )
-
-    def up_grad_copy(j):
-        return remote(send_u.at[(layer + j) % layers], got_u.at[j], v_sem, (j,), in_line(j))
-
-    for j in range(1, layers):
-        up_copy(j).start()
+    def grad_copy(k):
+        return remote(send_g.at[k], got_g.at[k], g_sem, (k,), pair * PLANE + column)
+
+    def far_copy(k):
+        return remote(far_g.at[k], in_g.at[k], h_sem, (k,), far * PLANE + column)
+
+    def up_grad_copy():
+        return remote(send_u, got_u, v_sem, (0,), pair * PLANE + column)
+
+    def up_far_copy():
+        return remote(far_u, in_u, w_sem, (0,), far * PLANE + column)
+
+    def hand(ref, sems, at):
+        return pltpu.make_async_remote_copy(
+            src_ref=ref,
+            dst_ref=ref,
+            send_sem=sems.at[(0,) + at],
+            recv_sem=sems.at[(1,) + at],
+            device_id=across,
+            device_id_type=MESH,
+        )
+
+    def hand_down(k, j):
+        return hand(all_down.at[k, (layer - j + layers) % layers], x_sem, (k, j))
+
+    def hand_up(j):
+        return hand(all_up.at[(layer - j + layers) % layers], y_sem, (j,))
+
+    def pass_down(k):
+        @pl.when(carrier)
+        def _():
+            for j in range(1, layers):
+                down_copy(k, j).wait_recv()
+                hand_down(k, j).start()
+
+    @pl.when(carrier)
+    def _():
+        for j in range(1, layers):
+            up_copy(j).start()
 
     starts = slot_starts(clips_ref, me * clip_count, clip_count, clip_rows, layers, block)
     slot = lax.broadcasted_iota(jnp.int32, (slots, rows), 0)
@@ -245,8 +294,11 @@
 
     @pl.loop(0, chunks)
     def _(k):
-        for j in range(1, layers):
-            down_copy(k, j).start()
+        @pl.when(carrier)
+        def _():
+            for j in range(1, layers):
+                down_copy(k, j).start()
+
         placed = dot(place[...], tokens_ref[:, span(k)]).astype(jnp.bfloat16)
         send_t[k] = placed.reshape(PLANE, block, width)
         for j in range(1, PLANE):
@@ -267,8 +319,20 @@
             preferred_element_type=jnp.float32,
         )
 
-    for j in range(1, layers):
-        up_copy(j).wait_recv()
+    @pl.when(carrier)
+    def _():
+        for j in range(1, layers):
+            up_copy(j).wait_recv()
+            hand_up(j).start()
+
+    for k in range(AHEAD):
+        pass_down(k)
+
+    @pl.when(jnp.logical_not(carrier))
+    def _():
+        for j in range(1, layers):
+            hand_up(j).wait_recv()
+
     for j in range(1, PLANE):
         value_copy(j).wait_recv()
 
@@ -286,10 +350,22 @@
     low_t[...] = jnp.where(own((all_rank, slots), 1, 0), full, 0.0).astype(jnp.bfloat16)
     acts[...] = jnp.zeros_like(acts)
 
+    def pass_grad(k):
+        grad_copy(k).wait_recv()
+        far_g[k] = (keep[k] + got_g[k, 1].astype(jnp.float32)).astype(jnp.bfloat16)
+        far_copy(k).start()
+
     @pl.loop(0, chunks)
     def _(k):
-        for j in range(1, layers):
-            down_copy(k, j).wait_recv()
+        @pl.when(k + AHEAD < chunks)
+        def _():
+            pass_down(k + AHEAD)
+
+        @pl.when(jnp.logical_not(carrier))
+        def _():
+            for j in range(1, layers):
+                hand_down(k, j).wait_recv()
+
         downs = all_down[k].reshape(all_rank, width)
         term = dot(low[...], downs).astype(jnp.bfloat16).reshape(PLANE, block, width)
         terms[k] = term
@@ -299,28 +375,29 @@
         for j in range(1, PLANE):
             token_copy(k, j).wait_recv()
         tokens = got_t[k].reshape(slots, width)
-        grad = dot(low_t[...], tokens).reshape(layers, rank, width)
-        send_g[k] = grad.astype(jnp.bfloat16)
-        for j in range(1, layers):
-            grad_copy(k, j).start()
-        down_grad_ref[:, span(k)] = lax.dot_general(
-            low_t[pl.ds(pl.multiple_of(layer * rank, rank), rank), :],
-            tokens,
-            (((1,), (0,)), ((), ())),
-            preferred_element_type=jnp.float32,
-        )
+        grad[...] = dot(low_t[...], tokens).reshape(layers, rank, width)
+        send_g[k, 0] = grad[pair].astype(jnp.bfloat16)
+        send_g[k, 1] = grad[pair_far].astype(jnp.bfloat16)
+        grad_copy(k).start()
+        down_grad_ref[:, span(k)] = grad[layer]
+        keep[k] = grad[far]
         acts[...] += lax.dot_general(downs, tokens, NT, preferred_element_type=jnp.float32)
 
+        @pl.when(k >= LAG)
+        def _():
+            pass_grad(k - LAG)
+
     acts_low = jnp.where(own((all_rank, slots), 1, 0), acts[...], 0.0).astype(jnp.bfloat16)
-    grad = dot(acts_low, got_c[...].reshape(slots, got_c.shape[2]))
-    base_u = grad.reshape(layers, rank, got_c.shape[2])
-    send_u[...] = base_u.astype(jnp.bfloat16)
-    for j in range(1, layers):
-        up_grad_copy(j).start()
-    mine = jnp.zeros((rank, got_c.shape[2]), jnp.float32)
-    for i in range(layers):
-        mine = jnp.where(layer == i, base_u[i], mine)
-    up_grad_ref[...] = mine
+    keep_u[...] = dot(acts_low, got_c[...].reshape(slots, got_c.shape[2])).reshape(keep_u.shape)
+    send_u[0] = keep_u[pair].astype(jnp.bfloat16)
+    send_u[1] = keep_u[pair_far].astype(jnp.bfloat16)
+    up_grad_copy().start()
+
+    for k in range(chunks - LAG, chunks):
+        pass_grad(k)
+    up_grad_copy().wait_recv()
+    far_u[...] = (keep_u[far] + got_u[1].astype(jnp.float32)).astype(jnp.bfloat16)
+    up_far_copy().start()
 
     @pl.loop(0, chunks)
     def _(k):
@@ -331,32 +408,42 @@
 
     @pl.loop(0, chunks)
     def _(k):
-        total = down_grad_ref[:, span(k)]
-        for j in range(1, layers):
-            grad_copy(k, j).wait_recv()
-            total = total + got_g[k, j].astype(jnp.float32)
-        down_grad_ref[:, span(k)] = total
-
-    total = up_grad_ref[...]
-    for j in range(1, layers):
-        up_grad_copy(j).wait_recv()
-        total = total + got_u[j].astype(jnp.float32)
-    up_grad_ref[...] = total
-
-    for j in range(1, layers):
-        up_copy(j).wait_send()
-        up_grad_copy(j).wait_send()
+        far_copy(k).wait_recv()
+        down_grad_ref[:, span(k)] = (
+            down_grad_ref[:, span(k)]
+            + got_g[k, 0].astype(jnp.float32)
+            + in_g[k].astype(jnp.float32)
+        )
+
+    up_far_copy().wait_recv()
+    up_grad_ref[...] = (
+        keep_u[layer] + got_u[0].astype(jnp.float32) + in_u[...].astype(jnp.float32)
+    )
+
+    up_grad_copy().wait_send()
+    up_far_copy().wait_send()
     for j in range(1, PLANE):
         value_copy(j).wait_send()
 
+    @pl.when(carrier)
+    def _():
+        for j in range(1, layers):
+            up_copy(j).wait_send()
+            hand_up(j).wait_send()
+
     @pl.loop(0, chunks)
     def _(k):
-        for j in range(1, layers):
-            down_copy(k, j).wait_send()
-            grad_copy(k, j).wait_send()
+        grad_copy(k).wait_send()
+        far_copy(k).wait_send()
         for j in range(1, PLANE):
             token_copy(k, j).wait_send()
             term_copy(k, j).wait_send()
+
+        @pl.when(carrier)
+        def _():
+            for j in range(1, layers):
+                down_copy(k, j).wait_send()
+                hand_down(k, j).wait_send()
 
 
 def fused(
@@ -402,10 +489,17 @@
             pltpu.VMEM((layers * rank, slots), jnp.float32),
             pltpu.VMEM((chunks, PLANE, block, width), half),
             pltpu.VMEM((chunks, PLANE, block, width), half),
-            pltpu.VMEM((chunks, layers, rank, width), half),
-            pltpu.VMEM((chunks, layers, rank, width), half),
-            pltpu.VMEM((layers, rank, value_width), half),
-            pltpu.VMEM((layers, rank, value_width), half),
+            pltpu.VMEM((layers, rank, width), jnp.float32),
+            pltpu.VMEM((chunks, rank, width), jnp.float32),
+            pltpu.VMEM((chunks, 2, rank, width), half),
+            pltpu.VMEM((chunks, 2, rank, width), half),
+            pltpu.VMEM((chunks, rank, width), half),
+            pltpu.VMEM((chunks, rank, width), half),
+            pltpu.VMEM((layers, rank, value_width), jnp.float32),
+            pltpu.VMEM((2, rank, value_width), half),
+            pltpu.VMEM((2, rank, value_width), half),
+            pltpu.VMEM((rank, value_width), half),
+            pltpu.VMEM((rank, value_width), half),
             pltpu.VMEM((chunks, rows, width), jnp.float32),
             dma(()),
             dma((2, chunks, PLANE)),
@@ -413,6 +507,10 @@
             dma((2, chunks, layers)),
             dma((2, layers)),
             dma((2, chunks, PLANE)),
+            dma((2, chunks)),
+            dma((2, chunks)),
+            dma((2, 1)),
+            dma((2, 1)),
             dma((2, chunks, layers)),
             dma((2, layers)),
         ],
@@ -434,7 +532,8 @@
 
 
 def solution(mesh):
-    body = fused if mesh.shape["tensor"] == 1 and mesh.shape["owner"] == 16 else shards
+    sizes = [mesh.shape[axis] for axis in ("groups", "owner", "tensor")]
+    body = fused if sizes == [2, 16, 1] else shards
     return jax.shard_map(
         body,
         mesh=mesh,

time: 128 us -> 95.2 us (0.74)
  Pallas kernels: 121 us -> 89.7 us
    pallas_call x1, Pallas kernels: 121 us -> 89.7 us  [fused(): pl.pallas_call(functools.partial(kernel, layers, clip_count, clip_rows, c...]
where the time goes in v2:
time: 95.2 us; the launch traced here: 95 us
  Pallas kernels  89.7 us (94%)
  local copies, waits for them, and re-layouts  4.59 us (5%)
    pallas_call x1, Pallas kernels, fused(): pl.pallas_call(functools.partial(kernel, layers, clip_count, clip_rows, c...  89.7 us
    unnamed x7, local copies, waits for them, and re-layouts  4.59 us

profile of v2, /device:TPU:1, one launch (start us, length us, event | category | flops | bytes accessed | tf_op | source)
XLA Modules:
  0.0 95.0 jit_solution(602413921777376040)
XLA Ops:
  0.6 89.7 %shard_map.85 = (bf16[192,4096]{1,0:T(8,128)(2,1)}, f32[64,4096]{1,0:T(8,128)}, f32[64,1024]{1,0:T(8,128)}) custom-call(s32[256]{0:T(256)} %clips_ref.1, bf16[192,4096]{1,0:T(8,128)(2,1)} %tokens_ref.1, bf16[192,1024]{1,0:T(8,128)(2,1)} %cotangent_ref.1, bf16[64,4096]{1,0:T(8,128)(2,1)} %bitcast.6, bf16[64,1024]{1,0:T(8,128)(2,1)} %bitcast.7, ...), custom_call_target="tpu_custom_call" | custom-call | flops 8000000000 | bytes 16777216 | tf_op jit(solution)/shard_map/pallas_call | solution.py:466
  90.4 0.0 copy-start
  90.4 2.8 %copy.12 = bf16[192,4096]{1,0:T(8,128)(2,1)} copy(bf16[192,4096]{1,0:T(8,128)(2,1)} %get-tuple-element.12) | data formatting | bytes 3145728
  93.2 0.0 copy-done
  93.2 0.0 copy-start.1
  93.2 1.0 %copy.13 = f32[1,64,4096]{2,1,0:T(8,128)} copy(f32[1,64,4096]{2,1,0:T(8,128)S(1)} %bitcast.4) | data formatting | bytes 2097152
  94.1 0.1 copy-done.1
  94.3 0.7 copy.14
Async XLA Ops:
  90.4 2.8 %copy-start = (f32[64,4096]{1,0:T(8,128)S(1)}, f32[64,4096]{1,0:T(8,128)}, u32[]{:S(2)}) copy-start(f32[64,4096]{1,0:T(8,128)} %get-tuple-element.7) | copy-start | bytes 3145732
  93.2 1.1 %copy-start.1 = (f32[64,1024]{1,0:T(8,128)S(1)}, f32[64,1024]{1,0:T(8,128)}, u32[]{:S(2)}) copy-start(f32[64,1024]{1,0:T(8,128)} %get-tuple-element.8) | copy-start | bytes 786436

commit v3 on v2

--- a/solution.py
+++ b/solution.py
@@ -85,6 +85,7 @@
 PLANE = 4
 AHEAD = 2
 LAG = 2
+HOLD = 5
 MESH = pl.DeviceIdType.MESH
 NT = (((1,), (1,)), ((), ()))
 
@@ -200,6 +201,17 @@
         pl.semaphore_signal(barrier, inc=1, device_id={"owner": in_line(j)}, device_id_type=MESH)
     across = {"groups": 1 - group, "owner": me}
     pl.semaphore_signal(barrier, inc=1, device_id=across, device_id_type=MESH)
+    starts = slot_starts(clips_ref, me * clip_count, clip_count, clip_rows, layers, block)
+    slot = lax.broadcasted_iota(jnp.int32, (slots, rows), 0)
+    target = placed_rows(starts, (slots, rows), 1, clip_rows)
+    place[...] = jnp.where(slot == target, 1.0, 0.0).astype(jnp.bfloat16)
+    slot = lax.broadcasted_iota(jnp.int32, (rows, slots), 1)
+    target = placed_rows(starts, (rows, slots), 0, clip_rows)
+    unplace[...] = jnp.where(slot == target, 1.0, 0.0).astype(jnp.bfloat16)
+
+    send_c[...] = (
+        dot(place[...], cotangent_ref[...]).astype(jnp.bfloat16).reshape(send_c.shape)
+    )
     pl.semaphore_wait(barrier, PLANE - 1 + layers - 1 + 1)
 
     def remote(src, dst, sems, at, owner):
@@ -278,17 +290,6 @@
         for j in range(1, layers):
             up_copy(j).start()
 
-    starts = slot_starts(clips_ref, me * clip_count, clip_count, clip_rows, layers, block)
-    slot = lax.broadcasted_iota(jnp.int32, (slots, rows), 0)
-    target = placed_rows(starts, (slots, rows), 1, clip_rows)
-    place[...] = jnp.where(slot == target, 1.0, 0.0).astype(jnp.bfloat16)
-    slot = lax.broadcasted_iota(jnp.int32, (rows, slots), 1)
-    target = placed_rows(starts, (rows, slots), 0, clip_rows)
-    unplace[...] = jnp.where(slot == target, 1.0, 0.0).astype(jnp.bfloat16)
-
-    send_c[...] = (
-        dot(place[...], cotangent_ref[...]).astype(jnp.bfloat16).reshape(send_c.shape)
-    )
     for j in range(1, PLANE):
         value_copy(j).start()
 
@@ -350,6 +351,10 @@
     low_t[...] = jnp.where(own((all_rank, slots), 1, 0), full, 0.0).astype(jnp.bfloat16)
     acts[...] = jnp.zeros_like(acts)
 
+    def send_terms(k):
+        for j in range(1, PLANE):
+            term_copy(k, j).start()
+
     def pass_grad(k):
         grad_copy(k).wait_recv()
         far_g[k] = (keep[k] + got_g[k, 1].astype(jnp.float32)).astype(jnp.bfloat16)
@@ -369,9 +374,13 @@
         downs = all_down[k].reshape(all_rank, width)
         term = dot(low[...], downs).astype(jnp.bfloat16).reshape(PLANE, block, width)
         terms[k] = term
-        for j in range(1, PLANE):
-            term_copy(k, j).start()
         back[k, column] = terms[k, column]
+
+        @pl.when(k >= HOLD)
+        def _():
+            send_terms(2 * (k - HOLD))
+            send_terms(2 * (k - HOLD) + 1)
+
         for j in range(1, PLANE):
             token_copy(k, j).wait_recv()
         tokens = got_t[k].reshape(slots, width)
@@ -386,6 +395,9 @@
         @pl.when(k >= LAG)
         def _():
             pass_grad(k - LAG)
+
+    for k in range(2 * (chunks - HOLD), chunks):
+        send_terms(k)
 
     acts_low = jnp.where(own((all_rank, slots), 1, 0), acts[...], 0.0).astype(jnp.bfloat16)
     keep_u[...] = dot(acts_low, got_c[...].reshape(slots, got_c.shape[2])).reshape(keep_u.shape)

time: 95.2 us -> 94.5 us (level)
  no operation moved by 1% of the time
where the time goes in v3:
time: 94.5 us; the launch traced here: 94.3 us
  Pallas kernels  89 us (94%)
  local copies, waits for them, and re-layouts  4.59 us (5%)
    pallas_call x1, Pallas kernels, fused(): pl.pallas_call(functools.partial(kernel, layers, clip_count, clip_rows, c...  89 us
    unnamed x7, local copies, waits for them, and re-layouts  4.59 us

profile of v3, /device:TPU:1, one launch (start us, length us, event | category | flops | bytes accessed | tf_op | source)
XLA Modules:
  0.0 94.3 jit_solution(2374497584410063300)
XLA Ops:
  0.6 89.0 %shard_map.85 = (bf16[192,4096]{1,0:T(8,128)(2,1)}, f32[64,4096]{1,0:T(8,128)}, f32[64,1024]{1,0:T(8,128)}) custom-call(s32[256]{0:T(256)} %clips_ref.1, bf16[192,4096]{1,0:T(8,128)(2,1)} %tokens_ref.1, bf16[192,1024]{1,0:T(8,128)(2,1)} %cotangent_ref.1, bf16[64,4096]{1,0:T(8,128)(2,1)} %bitcast.6, bf16[64,1024]{1,0:T(8,128)(2,1)} %bitcast.7, ...), custom_call_target="tpu_custom_call" | custom-call | flops 8000000000 | bytes 16777216 | tf_op jit(solution)/shard_map/pallas_call | solution.py:478
  89.7 0.0 copy-start
  89.7 2.8 %copy.12 = bf16[192,4096]{1,0:T(8,128)(2,1)} copy(bf16[192,4096]{1,0:T(8,128)(2,1)} %get-tuple-element.12) | data formatting | bytes 3145728
  92.5 0.0 copy-done
  92.5 0.0 copy-start.1
  92.5 1.0 %copy.13 = f32[1,64,4096]{2,1,0:T(8,128)} copy(f32[1,64,4096]{2,1,0:T(8,128)S(1)} %bitcast.4) | data formatting | bytes 2097152
  93.5 0.1 copy-done.1
  93.6 0.7 copy.14
Async XLA Ops:
  89.7 2.8 %copy-start = (f32[64,4096]{1,0:T(8,128)S(1)}, f32[64,4096]{1,0:T(8,128)}, u32[]{:S(2)}) copy-start(f32[64,4096]{1,0:T(8,128)} %get-tuple-element.7) | copy-start | bytes 3145732
  92.5 1.1 %copy-start.1 = (f32[64,1024]{1,0:T(8,128)S(1)}, f32[64,1024]{1,0:T(8,128)}, u32[]{:S(2)}) copy-start(f32[64,1024]{1,0:T(8,128)} %get-tuple-element.8) | copy-start | bytes 786436

commit v4 on v3

--- a/solution.py
+++ b/solution.py
@@ -123,11 +123,16 @@
     clip_rows,
     chunks,
     clips_ref,
-    tokens_ref,
+    tokens_hbm,
     cotangent_ref,
-    down_ref,
+    down_hbm,
     up_ref,
     frozen_ref,
+    out_hbm,
+    down_grad_hbm,
+    up_grad_hbm,
+    tokens_ref,
+    down_ref,
     out_ref,
     down_grad_ref,
     up_grad_ref,
@@ -157,6 +162,10 @@
     far_u,
     in_u,
     base,
+    in_sem,
+    out_sem,
+    grad_sem,
+    up_out_sem,
     frozen_sem,
     t_sem,
     c_sem,
@@ -186,7 +195,10 @@
     all_rank = layers * rank
 
     frozen_copy = pltpu.make_async_copy(frozen_ref, frozen, frozen_sem)
-    frozen_copy.start()
+    tokens_in = pltpu.make_async_copy(tokens_hbm, tokens_ref, in_sem.at[0])
+    down_in = pltpu.make_async_copy(down_hbm, down_ref, in_sem.at[1])
+    tokens_in.start()
+    down_in.start()
 
     def in_plane(j):
         return layer * PLANE + (column + j) % PLANE
@@ -205,9 +217,6 @@
     slot = lax.broadcasted_iota(jnp.int32, (slots, rows), 0)
     target = placed_rows(starts, (slots, rows), 1, clip_rows)
     place[...] = jnp.where(slot == target, 1.0, 0.0).astype(jnp.bfloat16)
-    slot = lax.broadcasted_iota(jnp.int32, (rows, slots), 1)
-    target = placed_rows(starts, (rows, slots), 0, clip_rows)
-    unplace[...] = jnp.where(slot == target, 1.0, 0.0).astype(jnp.bfloat16)
 
     send_c[...] = (
         dot(place[...], cotangent_ref[...]).astype(jnp.bfloat16).reshape(send_c.shape)
@@ -293,6 +302,10 @@
     for j in range(1, PLANE):
         value_copy(j).start()
 
+    tokens_in.wait()
+    down_in.wait()
+    frozen_copy.start()
+
     @pl.loop(0, chunks)
     def _(k):
         @pl.when(carrier)
@@ -307,6 +320,9 @@
         got_t[k, column] = send_t[k, column]
         all_down[k, layer] = down_ref[:, span(k)]
 
+    slot = lax.broadcasted_iota(jnp.int32, (rows, slots), 1)
+    target = placed_rows(starts, (rows, slots), 0, clip_rows)
+    unplace[...] = jnp.where(slot == target, 1.0, 0.0).astype(jnp.bfloat16)
     got_c[column] = send_c[column]
     all_up[layer] = up_ref[...]
     frozen_copy.wait()
@@ -411,12 +427,17 @@
     far_u[...] = (keep_u[far] + got_u[1].astype(jnp.float32)).astype(jnp.bfloat16)
     up_far_copy().start()
 
-    @pl.loop(0, chunks)
-    def _(k):
-        for j in range(1, PLANE):
-            term_copy(k, j).wait_recv()
-        returned = dot(unplace[...], back[k].reshape(slots, width))
-        out_ref[:, span(k)] = (base[k] + returned).astype(jnp.bfloat16)
+    def row_out(k):
+        return pltpu.make_async_copy(
+            out_ref.at[:, span(k)], out_hbm.at[:, span(k)], out_sem.at[k]
+        )
+
+    def grad_out(k):
+        return pltpu.make_async_copy(
+            down_grad_ref.at[:, span(k)], down_grad_hbm.at[:, span(k)], grad_sem.at[k]
+        )
+
+    up_out = pltpu.make_async_copy(up_grad_ref, up_grad_hbm, up_out_sem)
 
     @pl.loop(0, chunks)
     def _(k):
@@ -426,12 +447,23 @@
             + got_g[k, 0].astype(jnp.float32)
             + in_g[k].astype(jnp.float32)
         )
+        grad_out(k).start()
 
     up_far_copy().wait_recv()
     up_grad_ref[...] = (
         keep_u[layer] + got_u[0].astype(jnp.float32) + in_u[...].astype(jnp.float32)
     )
-
+    up_out.start()
+
+    @pl.loop(0, chunks)
+    def _(k):
+        for j in range(1, PLANE):
+            term_copy(k, j).wait_recv()
+        returned = dot(unplace[...], back[k].reshape(slots, width))
+        out_ref[:, span(k)] = (base[k] + returned).astype(jnp.bfloat16)
+        row_out(k).start()
+
+    up_out.wait()
     up_grad_copy().wait_send()
     up_far_copy().wait_send()
     for j in range(1, PLANE):
@@ -445,6 +477,8 @@
 
     @pl.loop(0, chunks)
     def _(k):
+        row_out(k).wait()
+        grad_out(k).wait()
         grad_copy(k).wait_send()
         far_copy(k).wait_send()
         for j in range(1, PLANE):
@@ -474,6 +508,7 @@
     slots = PLANE * block
     half = jnp.bfloat16
     vmem = pl.BlockSpec(memory_space=pltpu.VMEM)
+    anywhere = pl.BlockSpec(memory_space=pl.ANY)
     dma = pltpu.SemaphoreType.DMA
     out, down_grad, up_grad = pl.pallas_call(
         functools.partial(kernel, layers, clip_count, clip_rows, chunks),
@@ -482,11 +517,14 @@
             jax.ShapeDtypeStruct((rank, model_width), jnp.float32),
             jax.ShapeDtypeStruct((rank, value_width), jnp.float32),
         ),
-        in_specs=[pl.BlockSpec(memory_space=pltpu.SMEM)]
-        + [vmem] * 4
-        + [pl.BlockSpec(memory_space=pl.ANY)],
-        out_specs=(vmem, vmem, vmem),
+        in_specs=[pl.BlockSpec(memory_space=pltpu.SMEM), anywhere, vmem, anywhere, vmem, anywhere],
+        out_specs=(anywhere, anywhere, anywhere),
         scratch_shapes=[
+            pltpu.VMEM((rows, model_width), half),
+            pltpu.VMEM((rank, model_width), half),
+            pltpu.VMEM((rows, model_width), half),
+            pltpu.VMEM((rank, model_width), jnp.float32),
+            pltpu.VMEM((rank, value_width), jnp.float32),
             pltpu.VMEM((model_width, value_width), half),
             pltpu.VMEM((slots, rows), half),
             pltpu.VMEM((rows, slots), half),
@@ -513,6 +551,10 @@
             pltpu.VMEM((rank, value_width), half),
             pltpu.VMEM((rank, value_width), half),
             pltpu.VMEM((chunks, rows, width), jnp.float32),
+            dma((2,)),
+            dma((chunks,)),
+            dma((chunks,)),
+            dma(()),
             dma(()),
             dma((2, chunks, PLANE)),
             dma((2, PLANE)),

time: 94.5 us -> 92.8 us (0.982)
  Pallas kernels: 89 us -> 87.3 us
    pallas_call x1, Pallas kernels: 89 us -> 87.3 us  [fused(): pl.pallas_call(functools.partial(kernel, layers, clip_count, clip_rows, c...]
where the time goes in v4:
time: 92.8 us; the launch traced here: 92.5 us
  Pallas kernels  87.3 us (94%)
  local copies, waits for them, and re-layouts  4.59 us (5%)
    pallas_call x1, Pallas kernels, fused(): pl.pallas_call(functools.partial(kernel, layers, clip_count, clip_rows, c...  87.3 us
    unnamed x7, local copies, waits for them, and re-layouts  4.59 us

profile of v4, /device:TPU:1, one launch (start us, length us, event | category | flops | bytes accessed | tf_op | source)
XLA Modules:
  0.0 92.5 jit_solution(9741915299054297957)
XLA Ops:
  0.6 87.3 %shard_map.85 = (bf16[192,4096]{1,0:T(8,128)(2,1)}, f32[64,4096]{1,0:T(8,128)}, f32[64,1024]{1,0:T(8,128)}) custom-call(s32[256]{0:T(256)} %clips_ref.1, bf16[192,4096]{1,0:T(8,128)(2,1)} %tokens_hbm.1, bf16[192,1024]{1,0:T(8,128)(2,1)} %cotangent_ref.1, bf16[64,4096]{1,0:T(8,128)(2,1)} %bitcast.6, bf16[64,1024]{1,0:T(8,128)(2,1)} %bitcast.7, ...), custom_call_target="tpu_custom_call" | custom-call | flops 8000000000 | bytes 16777216 | tf_op jit(solution)/shard_map/pallas_call | solution.py:513
  87.9 0.0 copy-start
  87.9 2.8 %copy.12 = bf16[192,4096]{1,0:T(8,128)(2,1)} copy(bf16[192,4096]{1,0:T(8,128)(2,1)} %get-tuple-element.12) | data formatting | bytes 3145728
  90.7 0.0 copy-done
  90.7 0.0 copy-start.1
  90.7 1.0 %copy.13 = f32[1,64,4096]{2,1,0:T(8,128)} copy(f32[1,64,4096]{2,1,0:T(8,128)S(1)} %bitcast.4) | data formatting | bytes 2097152
  91.7 0.1 copy-done.1
  91.8 0.7 copy.14
Async XLA Ops:
  87.9 2.8 %copy-start = (f32[64,4096]{1,0:T(8,128)S(1)}, f32[64,4096]{1,0:T(8,128)}, u32[]{:S(2)}) copy-start(f32[64,4096]{1,0:T(8,128)} %get-tuple-element.7) | copy-start | bytes 3145732
  90.7 1.1 %copy-start.1 = (f32[64,1024]{1,0:T(8,128)S(1)}, f32[64,1024]{1,0:T(8,128)}, u32[]{:S(2)}) copy-start(f32[64,1024]{1,0:T(8,128)} %get-tuple-element.8) | copy-start | bytes 786436

commit v5 on v4

--- a/solution.py
+++ b/solution.py
@@ -84,8 +84,8 @@
 
 PLANE = 4
 AHEAD = 2
-LAG = 2
-HOLD = 5
+LAG = 1
+HOLD = 2
 MESH = pl.DeviceIdType.MESH
 NT = (((1,), (1,)), ((), ()))
 
@@ -502,7 +502,7 @@
     value_width = cotangent.shape[1]
     clip_rows = rows // clip_count
     rank = adapter_down_weight.shape[1]
-    chunks = 8
+    chunks = 4
     width = model_width // chunks
     block = layers * CAP * clip_rows
     slots = PLANE * block

time: 92.8 us -> 91.6 us (0.987)
  Pallas kernels: 87.3 us -> 86.1 us
    pallas_call x1, Pallas kernels: 87.3 us -> 86.1 us  [fused(): pl.pallas_call(functools.partial(kernel, layers, clip_count, clip_rows, c...]
where the time goes in v5:
time: 91.6 us; the launch traced here: 91.4 us
  Pallas kernels  86.1 us (94%)
  local copies, waits for them, and re-layouts  4.59 us (5%)
    pallas_call x1, Pallas kernels, fused(): pl.pallas_call(functools.partial(kernel, layers, clip_count, clip_rows, c...  86.1 us
    unnamed x7, local copies, waits for them, and re-layouts  4.59 us

profile of v5, /device:TPU:1, one launch (start us, length us, event | category | flops | bytes accessed | tf_op | source)
XLA Modules:
  0.0 91.4 jit_solution(6311222844160229074)
XLA Ops:
  0.6 86.1 %shard_map.85 = (bf16[192,4096]{1,0:T(8,128)(2,1)}, f32[64,4096]{1,0:T(8,128)}, f32[64,1024]{1,0:T(8,128)}) custom-call(s32[256]{0:T(256)} %clips_ref.1, bf16[192,4096]{1,0:T(8,128)(2,1)} %tokens_hbm.1, bf16[192,1024]{1,0:T(8,128)(2,1)} %cotangent_ref.1, bf16[64,4096]{1,0:T(8,128)(2,1)} %bitcast.6, bf16[64,1024]{1,0:T(8,128)(2,1)} %bitcast.7, ...), custom_call_target="tpu_custom_call" | custom-call | flops 8000000000 | bytes 16777216 | tf_op jit(solution)/shard_map/pallas_call | solution.py:513
  86.8 0.0 copy-start
  86.8 2.8 %copy.12 = bf16[192,4096]{1,0:T(8,128)(2,1)} copy(bf16[192,4096]{1,0:T(8,128)(2,1)} %get-tuple-element.12) | data formatting | bytes 3145728
  89.6 0.0 copy-done
  89.6 0.0 copy-start.1
  89.6 1.0 %copy.13 = f32[1,64,4096]{2,1,0:T(8,128)} copy(f32[1,64,4096]{2,1,0:T(8,128)S(1)} %bitcast.4) | data formatting | bytes 2097152
  90.5 0.1 copy-done.1
  90.7 0.7 copy.14
Async XLA Ops:
  86.8 2.8 %copy-start = (f32[64,4096]{1,0:T(8,128)S(1)}, f32[64,4096]{1,0:T(8,128)}, u32[]{:S(2)}) copy-start(f32[64,4096]{1,0:T(8,128)} %get-tuple-element.7) | copy-start | bytes 3145732
  89.6 1.1 %copy-start.1 = (f32[64,1024]{1,0:T(8,128)S(1)}, f32[64,1024]{1,0:T(8,128)}, u32[]{:S(2)}) copy-start(f32[64,1024]{1,0:T(8,128)} %get-tuple-element.8) | copy-start | bytes 786436

commit v6 on v5

--- a/solution.py
+++ b/solution.py
@@ -325,17 +325,6 @@
     unplace[...] = jnp.where(slot == target, 1.0, 0.0).astype(jnp.bfloat16)
     got_c[column] = send_c[column]
     all_up[layer] = up_ref[...]
-    frozen_copy.wait()
-
-    @pl.loop(0, chunks)
-    def _(k):
-        base[k] = lax.dot_general(
-            cotangent_ref[...],
-            frozen[span(k), :],
-            NT,
-            preferred_element_type=jnp.float32,
-        )
-
     @pl.when(carrier)
     def _():
         for j in range(1, layers):
@@ -420,6 +409,17 @@
     send_u[0] = keep_u[pair].astype(jnp.bfloat16)
     send_u[1] = keep_u[pair_far].astype(jnp.bfloat16)
     up_grad_copy().start()
+
+    frozen_copy.wait()
+
+    @pl.loop(0, chunks)
+    def _(k):
+        base[k] = lax.dot_general(
+            cotangent_ref[...],
+            frozen[span(k), :],
+            NT,
+            preferred_element_type=jnp.float32,
+        )
 
     for k in range(chunks - LAG, chunks):
         pass_grad(k)

time: 91.6 us -> 91.6 us (level)
  no operation moved by 1% of the time
where the time goes in v6:
time: 91.6 us; the launch traced here: 91.4 us
  Pallas kernels  86.1 us (94%)
  local copies, waits for them, and re-layouts  4.59 us (5%)
    pallas_call x1, Pallas kernels, fused(): pl.pallas_call(functools.partial(kernel, layers, clip_count, clip_rows, c...  86.1 us
    unnamed x7, local copies, waits for them, and re-layouts  4.59 us

profile of v6, /device:TPU:1, one launch (start us, length us, event | category | flops | bytes accessed | tf_op | source)
XLA Modules:
  0.0 91.4 jit_solution(15715849856524482870)
XLA Ops:
  0.6 86.1 %shard_map.85 = (bf16[192,4096]{1,0:T(8,128)(2,1)}, f32[64,4096]{1,0:T(8,128)}, f32[64,1024]{1,0:T(8,128)}) custom-call(s32[256]{0:T(256)} %clips_ref.1, bf16[192,4096]{1,0:T(8,128)(2,1)} %tokens_hbm.1, bf16[192,1024]{1,0:T(8,128)(2,1)} %cotangent_ref.1, bf16[64,4096]{1,0:T(8,128)(2,1)} %bitcast.6, bf16[64,1024]{1,0:T(8,128)(2,1)} %bitcast.7, ...), custom_call_target="tpu_custom_call" | custom-call | flops 8000000000 | bytes 16777216 | tf_op jit(solution)/shard_map/pallas_call | solution.py:513
  86.8 0.0 copy-start
  86.8 2.8 %copy.12 = bf16[192,4096]{1,0:T(8,128)(2,1)} copy(bf16[192,4096]{1,0:T(8,128)(2,1)} %get-tuple-element.12) | data formatting | bytes 3145728
  89.6 0.0 copy-done
  89.6 0.0 copy-start.1
  89.6 1.0 %copy.13 = f32[1,64,4096]{2,1,0:T(8,128)} copy(f32[1,64,4096]{2,1,0:T(8,128)S(1)} %bitcast.4) | data formatting | bytes 2097152
  90.5 0.1 copy-done.1
  90.7 0.7 copy.14
Async XLA Ops:
  86.8 2.8 %copy-start = (f32[64,4096]{1,0:T(8,128)S(1)}, f32[64,4096]{1,0:T(8,128)}, u32[]{:S(2)}) copy-start(f32[64,4096]{1,0:T(8,128)} %get-tuple-element.7) | copy-start | bytes 3145732
  89.6 1.1 %copy-start.1 = (f32[64,1024]{1,0:T(8,128)S(1)}, f32[64,1024]{1,0:T(8,128)}, u32[]{:S(2)}) copy-start(f32[64,1024]{1,0:T(8,128)} %get-tuple-element.8) | copy-start | bytes 786436
